TPU v7x, 256 devices: a whole 4x4x8 slice. The times are simulated.
256 devices in a mesh: row: 32 (over z, y), col: 8 (over x, core).
Axes of the slice: x: 4, y: 4, z: 8, core: 2. Of those that a mesh axis runs over, the one named last changes fastest.
Arguments:
- image: bfloat16 [16384, 512], P(('row', 'col')), may hold values from -2 to 2
- text: bfloat16 [16384, 512], P(('row', 'col')), may hold values from -3 to 3
- logit_scale: float32 [1], replicated, may hold values from 10 to 100
Outputs:
- loss: float32 [1], replicated
- grad_image: float32 [16384, 512], P(('row', 'col'))
- grad_text: float32 [16384, 512], P(('row', 'col'))
All inputs are finite; a program needn't handle non-finite values.
Results may differ from a plain program's by a relative error of at most 0.0095.
Values may be sent and summed in bfloat16 or wider, within the bound.
A program may use at most 64 MiB of HBM per device.

v0:
```python
import jax
import jax.numpy as jnp
from jax import lax
from jax.sharding import Mesh
from jax.sharding import PartitionSpec as P

COL = ("col_0", "col_1")
ROW = ("row_0", "row_1")
ROW_COL = ("row_0", "row_1", "col_0", "col_1")


def in_order(tiles, dim):
    tiles = jnp.moveaxis(tiles, 0, dim)
    dims = tiles.shape
    return tiles.reshape(*dims[:dim], dims[dim] * dims[dim + 1], *dims[dim + 2 :])


def from_everyone(value, axis):
    copies = jnp.broadcast_to(value, (lax.axis_size(axis), *value.shape))
    return lax.all_to_all(copies, axis, split_axis=0, concat_axis=0, tiled=True)


def gathered_copies(value, axis, dim):
    return in_order(from_everyone(value, axis), dim)


def gather_axes(value, axes, dim):
    for axis in reversed(axes):
        value = lax.all_gather(value, axis, axis=dim, tiled=True)
    return value


def all_in_one(value, axis):
    leaves = jax.tree.leaves(value)
    turns = sorted(range(len(leaves)), key=lambda k: -leaves[k].size)
    width = (1, *leaves[turns[0]].shape)[-1]
    lines = [
        jnp.pad(leaves[k].reshape(-1), (0, -leaves[k].size % width)).reshape(-1, width)
        for k in turns
    ]
    both, at, found = (from_everyone(jnp.concatenate(lines), axis), 0, {})
    for k, line in zip(turns, lines):
        share = both[:, at : at + len(line)].reshape(len(both), -1)
        found[k] = share[:, : leaves[k].size].reshape(-1, *leaves[k].shape)
        at += len(line)
    numbers = iter(range(len(leaves)))
    return jax.tree.map(lambda _: found[next(numbers)], value)


def joined_by_halves(pieces, combine):
    while len(jax.tree.leaves(pieces)[0]) > 1:
        pieces = jax.vmap(combine)(
            *(jax.tree.map(lambda part: part[side::2], pieces) for side in (0, 1))
        )
    return jax.tree.map(lambda part: part[0], pieces)


def combined_all(value, axis, combine):
    pieces = all_in_one(value, axis)
    return joined_by_halves(pieces, combine)


def all_in_one_2(value, axis):
    leaves = jax.tree.leaves(value)
    turns = sorted(range(len(leaves)), key=lambda k: -leaves[k].size)
    width = (1, *leaves[turns[0]].shape)[-1]
    lines = [
        jnp.pad(leaves[k].reshape(-1), (0, -leaves[k].size % width)).reshape(-1, width)
        for k in turns
    ]
    both, at, found = (lax.all_gather(jnp.concatenate(lines), axis), 0, {})
    for k, line in zip(turns, lines):
        share = both[:, at : at + len(line)].reshape(len(both), -1)
        found[k] = share[:, : leaves[k].size].reshape(-1, *leaves[k].shape)
        at += len(line)
    numbers = iter(range(len(leaves)))
    return jax.tree.map(lambda _: found[next(numbers)], value)


def merged_by_axis(value, axes, combine):
    for axis in axes:
        pieces = all_in_one_2(value, axis)
        value = jax.tree.map(lambda part: part[0], pieces)
        for k in range(1, lax.axis_size(axis)):
            value = combine(value, jax.tree.map(lambda part: part[k], pieces))
    return value


def over_axes(value, axes):
    for axis in axes:
        value = lax.psum(value, axis)
    return value


def sum_by_axis(total, axes):
    for axis in axes:
        total = lax.psum_scatter(total, axis, scatter_dimension=0, tiled=True)
    return total


def in_blocks(value, dim, count):
    dims = value.shape
    tiles = value.reshape(*dims[:dim], count, dims[dim] // count, *dims[dim + 1 :])
    return jnp.moveaxis(tiles, dim, 0)


def summed_on_arrival(value, axis, dim):
    count = lax.axis_size(axis)
    tiles = lax.all_to_all(in_blocks(value, dim, count), axis, 0, 0, tiled=True)
    return jnp.sum(tiles, axis=0)


def normalize(embedding):
    values = embedding.astype(jnp.float32)
    length = jnp.sqrt(jnp.sum(values * values, axis=1, keepdims=True) + 1e-06)
    return (values / length, length)


def unnormalize(unit_rows, length, gradient):
    return (gradient - unit_rows * jnp.sum(unit_rows * gradient, axis=1, keepdims=True)) / length


def combine(former, latter):
    summit = jnp.maximum(former[0], latter[0])
    return (
        summit,
        former[1] * jnp.exp(former[0] - summit) + latter[1] * jnp.exp(latter[0] - summit),
    )


def on_device(image, text, logit_scale):
    sharpness = logit_scale[0]
    unit_image, image_len = normalize(image)
    unit_text, text_len = normalize(text)
    img_own = unit_image.astype(jnp.bfloat16)
    txt_own = unit_text.astype(jnp.bfloat16)
    img_tile = gathered_copies(img_own, COL, 0)
    txt_tile = gather_axes(txt_own, ROW, 0)
    columns = txt_tile.shape[0]
    block_cols = min(512, columns)
    block_count = columns // block_cols
    txt_blocks = txt_tile.reshape(block_count, block_cols, txt_tile.shape[1])

    def scores(txt_block):
        return sharpness * jnp.einsum(
            "re,ce->rc", img_tile, txt_block, preferred_element_type=jnp.float32
        )

    lowest = jnp.full((img_tile.shape[0],), -1e30, jnp.float32)

    def online(running, txt_block):
        row_peak, row_sum = running
        logits = scores(txt_block)
        col_peak = jnp.max(logits, axis=0)
        col_sum = jnp.sum(jnp.exp(logits - col_peak[None, :]), axis=0)
        higher = jnp.maximum(row_peak, jnp.max(logits, axis=1))
        row_sum = row_sum * jnp.exp(row_peak - higher) + jnp.sum(
            jnp.exp(logits - higher[:, None]), axis=1
        )
        return ((higher, row_sum), (col_peak, col_sum))

    (row_peak, row_sum), (col_peak, col_sum) = lax.scan(
        online, (lowest, jnp.zeros_like(lowest)), txt_blocks
    )
    row_peak, row_sum = combined_all((row_peak, row_sum), COL, combine)
    col_peak, col_sum = merged_by_axis((col_peak.reshape(-1), col_sum.reshape(-1)), ROW, combine)
    row_lse = row_peak + jnp.log(row_sum)
    col_lse = col_peak + jnp.log(col_sum)
    own_rows = image.shape[0]
    row_mine = lax.dynamic_slice_in_dim(row_lse, lax.axis_index(COL) * own_rows, own_rows)
    col_mine = lax.dynamic_slice_in_dim(col_lse, lax.axis_index(ROW) * own_rows, own_rows)
    img_wide = img_own.astype(jnp.float32)
    txt_wide = txt_own.astype(jnp.float32)
    positive = sharpness * jnp.sum(img_wide * txt_wide, axis=1)
    partial_value = jnp.sum(row_mine - positive) + jnp.sum(col_mine - positive)
    overall = over_axes(partial_value, ROW_COL)
    batch_size = own_rows * lax.axis_size(ROW) * lax.axis_size(COL)
    loss = (overall / (2 * batch_size)).reshape(1)

    def weights_of(txt_block, lse_cols):
        logits = scores(txt_block)
        return (
            0.5 * (jnp.exp(logits - row_lse[:, None]) + jnp.exp(logits - lse_cols[None, :]))
        ).astype(jnp.bfloat16)

    start_grad = jnp.zeros((img_tile.shape[0], img_tile.shape[1]), jnp.float32)
    lse_blocks = col_lse.reshape(block_count, block_cols)

    def keep_weights(running, inputs):
        txt_block, lse_cols = inputs
        weights = weights_of(txt_block, lse_cols)
        running = running + sharpness * jnp.dot(
            weights, txt_block, preferred_element_type=jnp.float32
        )
        return (running, weights)

    img_terms, stored = lax.scan(keep_weights, start_grad, (txt_blocks, lse_blocks))
    flipped = jnp.swapaxes(stored, 1, 2).reshape(columns, img_tile.shape[0])
    txt_grad = sum_by_axis(
        sharpness * jnp.dot(flipped, img_tile, preferred_element_type=jnp.float32), ROW
    )
    img_grad = summed_on_arrival(img_terms, COL, 0)
    img_grad = img_grad - sharpness * txt_wide
    txt_grad = txt_grad - sharpness * img_wide
    return (
        loss,
        unnormalize(unit_image, image_len, img_grad),
        unnormalize(unit_text, text_len, txt_grad),
    )


def solution(mesh):
    torus = Mesh(mesh.devices.reshape(8, 4, 4, 2), ("row_0", "row_1", "col_0", "col_1"))
    return jax.shard_map(
        on_device,
        mesh=torus,
        in_specs=(P(ROW_COL, None), P(ROW_COL, None), P()),
        out_specs=(P(), P(ROW_COL, None), P(ROW_COL, None)),
        check_vma=False,
    )
```

profile of v0, /device:TPU:1, one launch (start us, length us, event | category | flops | bytes accessed | tf_op | source)
XLA Modules:
  0.0 286.2 jit_solution(1497360225404504215)
XLA Ops:
  7.2 1.0 fusion.11
  8.2 0.9 fusion.58
  9.1 11.9 %all_gather.18 = bf16[256,512]{1,0:T(8,128)(2,1)} all-gather(bf16[64,512]{1,0:T(8,128)(2,1)S(1)} %fusion.58), channel_id=1, replica_groups=mesh['row_0'=8,'row_1'=4,'col_0'=4,'col_1'=2] {'row_1'}, dimensions={0}, use_global_device_ids=true | all-gather | bytes 327680 | tf_op jit(solution)/shard_map/all_gather | solution.py:29
  21.1 1.0 fusion.12
  22.0 0.9 fusion.59
  23.0 0.8 broadcast_in_dim.39
  23.8 8.4 %all-to-all-start = ((bf16[8,64,512]{2,1,0:T(8,128)(2,1)}), bf16[8,64,512]{2,1,0:T(8,128)(2,1)}, u32[]{:S(2)}, u32[]{:S(2)}) async-start(bf16[8,64,512]{2,1,0:T(8,128)(2,1)} %broadcast_in_dim.39), calls=%async_computation | async-start | bytes 1048576 | tf_op jit(solution)/shard_map/all_to_all | solution.py:20
  32.8 8.9 %all-to-all-done = bf16[8,64,512]{2,1,0:T(8,128)(2,1)} async-done(((bf16[8,64,512]{2,1,0:T(8,128)(2,1)}), bf16[8,64,512]{2,1,0:T(8,128)(2,1)}, u32[]{:S(2)}, u32[]{:S(2)}) %all-to-all-start) | async-done | bytes 524320 | tf_op jit(solution)/shard_map/all_to_all | solution.py:20
  41.8 21.7 %all-gather.6.cloned.1.call-done = bf16[2048,512]{1,0:T(8,128)(2,1)} async-done(((bf16[256,512]{1,0:T(8,128)(2,1)}), bf16[2048,512]{1,0:T(8,128)(2,1)}) %all-gather.6.cloned.1.call-update) | async-done | bytes 2097168 | tf_op jit(solution)/shard_map/all_gather | solution.py:29
  63.5 11.7 %while.30 = (s32[]{:T(128)}, f32[512]{0:T(512)S(1)}, f32[512]{0:T(512)S(1)}, f32[4,512]{1,0:T(4,128)S(1)}, f32[4,512]{1,0:T(4,128)S(1)}, /*index=5*/f32[]{:T(128...) while((s32[]{:T(128)}, f32[512]{0:T(512)S(1)}, ...), condition=%wide.region_7.8_spmd.clone, body=%wide.region_2.7_spmd.clone.sunk | while | flops 270272000 | bytes 3187832 | solution.py:162
  63.5 2.4 fusion.77
  65.9 0.4 exponential_reduce_fusion.3
  66.3 0.1 dynamic_update_slice.18
  66.4 2.4 fusion.77
  68.8 0.4 exponential_reduce_fusion.3
  69.4 2.4 fusion.77
  71.8 0.4 exponential_reduce_fusion.3
  72.3 2.4 fusion.77
  74.7 0.4 exponential_reduce_fusion.3
  75.3 18.5 %all-gather.2 = f32[8,2,2048]{2,1,0:T(2,128)S(1)} all-gather(f32[1,2,2048]{2,1,0:T(2,128)S(1)} %maximum_bitcast_fusion), channel_id=2, replica_groups=mesh['row_0'=8,'row_1'=4,'col_0'=4,'col_1'=2] {'row_0'}, dimensions={0}, use_global_device_ids=true | all-gather | bytes 147456 | tf_op jit(solution)/shard_map/all_gather | solution.py:71
  93.8 0.2 fusion.17
  94.0 9.4 %all-gather.3 = f32[4,2,2048]{2,1,0:T(2,128)S(1)} all-gather(f32[1,2,2048]{2,1,0:T(2,128)S(1)} %maximum_bitcast_fusion.1), channel_id=3, replica_groups=mesh['row_0'=8,'row_1'=4,'col_0'=4,'col_1'=2] {'row_1'}, dimensions={0}, use_global_device_ids=true | all-gather | bytes 81920 | tf_op jit(solution)/shard_map/all_gather | solution.py:71
  103.4 0.2 slice_reduce_fusion.3
  103.7 0.6 broadcast_in_dim.40
  104.3 17.5 %all-to-all-start.1 = ((f32[8,2,512]{2,1,0:T(2,128)}), f32[8,2,512]{2,1,0:T(2,128)S(1)}, u32[]{:S(2)}, u32[]{:S(2)}) async-start(f32[8,2,512]{2,1,0:T(2,128)} %broadcast_in_dim.40), calls=%async_computation.1 | async-start | bytes 65536 | tf_op jit(solution)/shard_map/all_to_all | solution.py:20
  121.9 4.7 %all-to-all-done.1 = f32[8,2,512]{2,1,0:T(2,128)S(1)} async-done(((f32[8,2,512]{2,1,0:T(2,128)}), f32[8,2,512]{2,1,0:T(2,128)S(1)}, u32[]{:S(2)}, u32[]{:S(2)}) %all-to-all-start.1) | async-done | bytes 32800 | tf_op jit(solution)/shard_map/all_to_all | solution.py:20
  126.9 23.7 %while.31 = (s32[]{:T(128)}, f32[512,512]{1,0:T(8,128)}, bf16[4,512,512]{1,2,0:T(8,128)(2,1)S(1)}, f32[]{:T(128)}, bf16[4,512,512]{2,1,0:T(8,128)(2,1)}, /*index...) while((s32[]{:T(128)}, f32[512,512]{1,0:T(8,128)}, ...), condition=%wide.region_16.17_spmd.clone, body=%wide.region_15.16_spmd.clone.sunk | while | flops 539230208 | bytes 5253747 | solution.py:197
  126.9 2.5 bitcast_dynamic-update-slice_fusion.2
  129.4 3.1 %fusion.82 = f32[512,512]{1,0:T(8,128)} fusion(bf16[512,512]{1,0:T(8,128)(2,1)S(1)} %get-tuple-element.337, f32[512,512]{1,0:T(8,128)} %get-tuple-element.380, f32[]{:T(128)} %get-tuple-element.392, pred[]{:T(512)S(6)} %compare.7, bf16[4,512,512]{2,1,0:T(8,128)(2,1)} %get-tuple-element.393, s32[]{:T(128)} %get-tuple-element.379), kind=kOutput, calls=%fused_computation.10.clone.1 | convolution fusion | flops 269221888 | bytes 3146753 | tf_op jit(solution)/shard_map/while/body/eval_jaxpr/dot_general | solution.py:192
  132.6 2.5 bitcast_dynamic-update-slice_fusion.2
  135.1 3.5 %fusion.82 = f32[512,512]{1,0:T(8,128)} fusion(bf16[512,512]{1,0:T(8,128)(2,1)S(1)} %get-tuple-element.337, f32[512,512]{1,0:T(8,128)} %get-tuple-element.380, f32[]{:T(128)} %get-tuple-element.392, pred[]{:T(512)S(6)} %compare.7, bf16[4,512,512]{2,1,0:T(8,128)(2,1)} %get-tuple-element.393, s32[]{:T(128)} %get-tuple-element.379), kind=kOutput, calls=%fused_computation.10.clone.1 | convolution fusion | flops 269221888 | bytes 3146753 | tf_op jit(solution)/shard_map/while/body/eval_jaxpr/dot_general | solution.py:192
  138.6 2.5 bitcast_dynamic-update-slice_fusion.2
  141.1 3.5 %fusion.82 = f32[512,512]{1,0:T(8,128)} fusion(bf16[512,512]{1,0:T(8,128)(2,1)S(1)} %get-tuple-element.337, f32[512,512]{1,0:T(8,128)} %get-tuple-element.380, f32[]{:T(128)} %get-tuple-element.392, pred[]{:T(512)S(6)} %compare.7, bf16[4,512,512]{2,1,0:T(8,128)(2,1)} %get-tuple-element.393, s32[]{:T(128)} %get-tuple-element.379), kind=kOutput, calls=%fused_computation.10.clone.1 | convolution fusion | flops 269221888 | bytes 3146753 | tf_op jit(solution)/shard_map/while/body/eval_jaxpr/dot_general | solution.py:192
  144.6 2.5 bitcast_dynamic-update-slice_fusion.2
  147.1 3.5 %fusion.82 = f32[512,512]{1,0:T(8,128)} fusion(bf16[512,512]{1,0:T(8,128)(2,1)S(1)} %get-tuple-element.337, f32[512,512]{1,0:T(8,128)} %get-tuple-element.380, f32[]{:T(128)} %get-tuple-element.392, pred[]{:T(512)S(6)} %compare.7, bf16[4,512,512]{2,1,0:T(8,128)(2,1)} %get-tuple-element.393, s32[]{:T(128)} %get-tuple-element.379), kind=kOutput, calls=%fused_computation.10.clone.1 | convolution fusion | flops 269221888 | bytes 3146753 | tf_op jit(solution)/shard_map/while/body/eval_jaxpr/dot_general | solution.py:192
  150.6 4.2 %convolution_multiply_fusion.3 = f32[2048,512]{1,0:T(8,128)} fusion(bf16[2048,512]{1,0:T(8,128)(2,1)S(1)} %bitcast.243, bf16[512,512]{1,0:T(8,128)(2,1)} %bitcast.2, f32[]{:T(128)} %bitcast.241), kind=kOutput, calls=%fused_computation.21 | convolution fusion | flops 1074790400 | bytes 6815748 | tf_op jit(solution)/shard_map/dot_general | solution.py:200
  154.9 51.6 %reduce-scatter.3.cloned.1.call-done = f32[256,512]{1,0:T(8,128)} async-done(((f32[2048,512]{1,0:T(8,128)}), f32[256,512]{1,0:T(8,128)}) %reduce-scatter.3.cloned.1.call-update) | async-done | bytes 524304 | tf_op jit(solution)/shard_map/reduce_scatter | solution.py:97
  206.5 4.9 %all-to-all-start.2 = ((f32[8,64,512]{2,1,0:T(8,128)}), f32[8,64,512]{2,1,0:T(8,128)S(1)}, u32[]{:S(2)}, u32[]{:S(2)}) async-start(f32[8,64,512]{2,1,0:T(8,128)} %bitcast.35), calls=%async_computation.2 | async-start | bytes 2097152 | tf_op jit(solution)/shard_map/all_to_all | solution.py:109
  211.4 15.1 %all-to-all-done.2 = f32[8,64,512]{2,1,0:T(8,128)S(1)} async-done(((f32[8,64,512]{2,1,0:T(8,128)}), f32[8,64,512]{2,1,0:T(8,128)S(1)}, u32[]{:S(2)}, u32[]{:S(2)}) %all-to-all-start.2) | async-done | bytes 1048608 | tf_op jit(solution)/shard_map/all_to_all | solution.py:109
  226.5 0.1 reduce_sum.95
  226.6 3.4 %reduce-scatter.5.cloned.1.call-done = f32[64,512]{1,0:T(8,128)} async-done(((f32[256,512]{1,0:T(8,128)}), f32[64,512]{1,0:T(8,128)}) %reduce-scatter.5.cloned.1.call-update) | async-done | bytes 131088 | tf_op jit(solution)/shard_map/reduce_scatter | solution.py:97
  230.0 1.2 multiply_reduce_fusion
  231.2 0.7 subtract_reduce_fusion
  233.2 14.2 %psum.28 = f32[]{:T(128)} all-reduce(f32[]{:T(128)S(6)} %add.191), channel_id=1, replica_groups=mesh['row_0'=8,'row_1'=4,'col_0'=4,'col_1'=2] {'row_0'}, use_global_device_ids=true, to_apply=%region_11.12 | all-reduce | flops 1 | bytes 8 | tf_op jit(solution)/shard_map/psum | solution.py:91
  247.4 7.5 %psum.29 = f32[]{:T(128)} all-reduce(f32[]{:T(128)} %psum.28), channel_id=1, replica_groups=mesh['row_0'=8,'row_1'=4,'col_0'=4,'col_1'=2] {'row_1'}, use_global_device_ids=true, to_apply=%region_12.13 | all-reduce | flops 1 | bytes 8 | tf_op jit(solution)/shard_map/psum | solution.py:91
  254.9 9.0 %psum.30 = f32[]{:T(128)} all-reduce(f32[]{:T(128)} %psum.29), channel_id=1, replica_groups=mesh['row_0'=8,'row_1'=4,'col_0'=4,'col_1'=2] {'col_0'}, use_global_device_ids=true, to_apply=%region_13.14 | all-reduce | flops 1 | bytes 8 | tf_op jit(solution)/shard_map/psum | solution.py:91
  263.8 12.3 %psum.31 = f32[]{:T(128)} all-reduce(f32[]{:T(128)} %psum.30), channel_id=1, replica_groups=mesh['row_0'=8,'row_1'=4,'col_0'=4,'col_1'=2] {'col_1'}, use_global_device_ids=true, to_apply=%region_14.15 | all-reduce | flops 1 | bytes 8 | tf_op jit(solution)/shard_map/psum | solution.py:91
  276.8 1.7 subtract_divide_fusion
  (71 shorter events, 1.1 us)
Async XLA Ops:
  7.2 56.3 %all-gather.6.cloned.1.call-start = ((), (), s32[]{:S(2)}) async-start(), calls=%async_computation.5 | async-start | bytes 2359296 | tf_op jit(solution)/shard_map/all_gather | solution.py:29
  23.8 18.0 %all-to-all-start = ((bf16[8,64,512]{2,1,0:T(8,128)(2,1)}), bf16[8,64,512]{2,1,0:T(8,128)(2,1)}, u32[]{:S(2)}, u32[]{:S(2)}) async-start(bf16[8,64,512]{2,1,0:T(8,128)(2,1)} %broadcast_in_dim.39), calls=%async_computation | async-start | bytes 1048576 | tf_op jit(solution)/shard_map/all_to_all | solution.py:20
  104.3 22.2 %all-to-all-start.1 = ((f32[8,2,512]{2,1,0:T(2,128)}), f32[8,2,512]{2,1,0:T(2,128)S(1)}, u32[]{:S(2)}, u32[]{:S(2)}) async-start(f32[8,2,512]{2,1,0:T(2,128)} %broadcast_in_dim.40), calls=%async_computation.1 | async-start | bytes 65536 | tf_op jit(solution)/shard_map/all_to_all | solution.py:20
  121.8 84.7 %reduce-scatter.3.cloned.1.call-start = ((), (), s32[]{:S(2)}) async-start(), calls=%async_computation.6 | async-start | bytes 4718592 | tf_op jit(solution)/shard_map/reduce_scatter | solution.py:97
  154.8 75.1 %copy-start = (bf16[64,512]{1,0:T(8,128)(2,1)S(1)}, bf16[64,512]{1,0:T(8,128)(2,1)}, u32[]{:S(2)}) copy-start(bf16[64,512]{1,0:T(8,128)(2,1)} %param.8) | copy-start | bytes 196612
  154.8 75.1 %copy-start.1 = (bf16[64,512]{1,0:T(8,128)(2,1)S(1)}, bf16[64,512]{1,0:T(8,128)(2,1)}, u32[]{:S(2)}) copy-start(bf16[64,512]{1,0:T(8,128)(2,1)} %param.7) | copy-start | bytes 196612
  154.9 75.1 %reduce-scatter.5.cloned.1.call-start = ((), (), s32[]{:S(2)}) async-start(), calls=%async_computation.7 | async-start | bytes 655360 | tf_op jit(solution)/shard_map/reduce_scatter | solution.py:97
  206.5 20.0 %all-to-all-start.2 = ((f32[8,64,512]{2,1,0:T(8,128)}), f32[8,64,512]{2,1,0:T(8,128)S(1)}, u32[]{:S(2)}, u32[]{:S(2)}) async-start(f32[8,64,512]{2,1,0:T(8,128)} %bitcast.35), calls=%async_computation.2 | async-start | bytes 2097152 | tf_op jit(solution)/shard_map/all_to_all | solution.py:109
Sparse Core Ops, SparseCore 0:
  21.2 42.2 all-gather.5
  155.0 51.5 reduce-scatter.2
  209.1 20.8 reduce-scatter.4
where the time goes:
time: 287 us; the launch traced here: 286 us
  waiting for transfers between devices  105 us (37%)
  blocking collectives  82.8 us (29%)
  matrix products  37.4 us (13%)
  starting transfers between devices  30.8 us (11%)
  between operations  17.6 us (6%)
  other arithmetic  9.43 us (3%)
    reduce_scatter x2, waiting for transfers between devices, sum_by_axis(): total = lax.psum_scatter(total, axis, scatter_dimension=0, tiled=True)  55 us
    psum x4, blocking collectives, over_axes(): value = lax.psum(value, axis)  43 us
    all_gather x2, blocking collectives, all_in_one_2(): both, at, found = (lax.all_gather(jnp.concatenate(lines), axis), 0, {})  27.9 us
    all_to_all x2, starting transfers between devices, from_everyone(): return lax.all_to_all(copies, axis, split_axis=0, concat_axis=0, tiled=True)  25.9 us
    all_gather x1, waiting for transfers between devices, gather_axes(): value = lax.all_gather(value, axis, axis=dim, tiled=True)  21.7 us
    dot_general x8, matrix products, scores(): jnp.einsum('re,ce->rc', img_tile, txt_block, preferred_element_type=jnp.f...  19.6 us
    all_to_all x1, waiting for transfers between devices, summed_on_arrival(): tiles = lax.all_to_all(in_blocks(value, dim, count), axis, 0, 0, tiled=True)  15.1 us
    all_to_all x2, waiting for transfers between devices, from_everyone(): return lax.all_to_all(copies, axis, split_axis=0, concat_axis=0, tiled=True)  13.6 us
  transfers between devices with their start and end apart: 6, of which 6 were waited for; matrix products, arithmetic and copies ran while one was open for 1% of the time, Pallas kernels for 0%

commit v1 on v0

--- a/solution.py
+++ b/solution.py
@@ -7,6 +7,11 @@
 COL = ("col_0", "col_1")
 ROW = ("row_0", "row_1")
 ROW_COL = ("row_0", "row_1", "col_0", "col_1")
+
+
+def pass_the_trails(z_in, device_axis):
+    piece_out = jax.lax.all_gather(z_in, device_axis).sum(axis=0)
+    return piece_out
 
 
 def in_order(tiles, dim):
@@ -88,7 +93,7 @@
 
 def over_axes(value, axes):
     for axis in axes:
-        value = lax.psum(value, axis)
+        value = pass_the_trails(value, axis)
     return value
 
 

time: 287 us -> 295 us (1.028)
  local copies, waits for them, and re-layouts: 2.4 us -> 9.72 us
  other arithmetic: 9.43 us -> 12.5 us
    psum x4 -> x0, blocking collectives: 43 us -> none  [over_axes(): value = lax.psum(value, axis)]
    unnamed x0 -> x4, blocking collectives: none -> 40.6 us
    unnamed x8 -> x26, local copies, waits for them, and re-layouts: 0.04 us -> 7.36 us
where the time goes in v1:
time: 295 us; the launch traced here: 294 us
  waiting for transfers between devices  105 us (36%)
  blocking collectives  80.4 us (27%)
  matrix products  37.4 us (13%)
  starting transfers between devices  31 us (11%)
  between operations  17.7 us (6%)
  other arithmetic  12.5 us (4%)
  local copies, waits for them, and re-layouts  9.72 us (3%)
    reduce_scatter x2, waiting for transfers between devices, sum_by_axis(): total = lax.psum_scatter(total, axis, scatter_dimension=0, tiled=True)  54.8 us
    unnamed x4, blocking collectives  40.6 us
    all_gather x2, blocking collectives, all_in_one_2(): both, at, found = (lax.all_gather(jnp.concatenate(lines), axis), 0, {})  27.9 us
    all_to_all x2, starting transfers between devices, from_everyone(): return lax.all_to_all(copies, axis, split_axis=0, concat_axis=0, tiled=True)  25.9 us
    all_gather x1, waiting for transfers between devices, gather_axes(): value = lax.all_gather(value, axis, axis=dim, tiled=True)  21.7 us
    dot_general x8, matrix products, scores(): jnp.einsum('re,ce->rc', img_tile, txt_block, preferred_element_type=jnp.f...  19.6 us
    all_to_all x1, waiting for transfers between devices, summed_on_arrival(): tiles = lax.all_to_all(in_blocks(value, dim, count), axis, 0, 0, tiled=True)  14.5 us
    all_to_all x2, waiting for transfers between devices, from_everyone(): return lax.all_to_all(copies, axis, split_axis=0, concat_axis=0, tiled=True)  13.6 us
  transfers between devices with their start and end apart: 6, of which 6 were waited for; matrix products, arithmetic and copies ran while one was open for 1% of the time, Pallas kernels for 0%

profile of v1, /device:TPU:1, one launch (start us, length us, event | category | flops | bytes accessed | tf_op | source)
XLA Modules:
  0.0 293.7 jit_solution(2715387670934187402)
XLA Ops:
  7.2 1.0 fusion.11
  8.2 0.9 fusion.58
  9.1 11.9 %all_gather.42 = bf16[256,512]{1,0:T(8,128)(2,1)} all-gather(bf16[64,512]{1,0:T(8,128)(2,1)S(1)} %fusion.58), channel_id=1, replica_groups=mesh['row_0'=8,'row_1'=4,'col_0'=4,'col_1'=2] {'row_1'}, dimensions={0}, use_global_device_ids=true | all-gather | bytes 327680 | tf_op jit(solution)/shard_map/all_gather | solution.py:34
  21.1 1.0 fusion.12
  22.0 0.9 fusion.59
  23.0 0.8 broadcast_in_dim.39
  23.8 8.4 %all-to-all-start = ((bf16[8,64,512]{2,1,0:T(8,128)(2,1)}), bf16[8,64,512]{2,1,0:T(8,128)(2,1)}, u32[]{:S(2)}, u32[]{:S(2)}) async-start(bf16[8,64,512]{2,1,0:T(8,128)(2,1)} %broadcast_in_dim.39), calls=%async_computation | async-start | bytes 1048576 | tf_op jit(solution)/shard_map/all_to_all | solution.py:25
  32.8 8.9 %all-to-all-done = bf16[8,64,512]{2,1,0:T(8,128)(2,1)} async-done(((bf16[8,64,512]{2,1,0:T(8,128)(2,1)}), bf16[8,64,512]{2,1,0:T(8,128)(2,1)}, u32[]{:S(2)}, u32[]{:S(2)}) %all-to-all-start) | async-done | bytes 524320 | tf_op jit(solution)/shard_map/all_to_all | solution.py:25
  41.8 21.7 %all-gather.6.cloned.1.call-done = bf16[2048,512]{1,0:T(8,128)(2,1)} async-done(((bf16[256,512]{1,0:T(8,128)(2,1)}), bf16[2048,512]{1,0:T(8,128)(2,1)}) %all-gather.6.cloned.1.call-update) | async-done | bytes 2097168 | tf_op jit(solution)/shard_map/all_gather | solution.py:34
  63.5 11.7 %while.30 = (s32[]{:T(128)}, f32[512]{0:T(512)S(1)}, f32[512]{0:T(512)S(1)}, f32[4,512]{1,0:T(4,128)S(1)}, f32[4,512]{1,0:T(4,128)S(1)}, /*index=5*/f32[]{:T(128...) while((s32[]{:T(128)}, f32[512]{0:T(512)S(1)}, ...), condition=%wide.region_7.8_spmd.clone, body=%wide.region_2.7_spmd.clone.sunk | while | flops 270272000 | bytes 3187832 | solution.py:167
  63.5 2.4 fusion.77
  66.4 2.4 fusion.77
  69.4 2.4 fusion.77
  72.3 2.4 fusion.77
  75.3 18.5 %all-gather.2 = f32[8,2,2048]{2,1,0:T(2,128)S(1)} all-gather(f32[1,2,2048]{2,1,0:T(2,128)S(1)} %maximum_bitcast_fusion), channel_id=2, replica_groups=mesh['row_0'=8,'row_1'=4,'col_0'=4,'col_1'=2] {'row_0'}, dimensions={0}, use_global_device_ids=true | all-gather | bytes 147456 | tf_op jit(solution)/shard_map/all_gather | solution.py:76
  94.0 9.4 %all-gather.3 = f32[4,2,2048]{2,1,0:T(2,128)S(1)} all-gather(f32[1,2,2048]{2,1,0:T(2,128)S(1)} %maximum_bitcast_fusion.1), channel_id=3, replica_groups=mesh['row_0'=8,'row_1'=4,'col_0'=4,'col_1'=2] {'row_1'}, dimensions={0}, use_global_device_ids=true | all-gather | bytes 81920 | tf_op jit(solution)/shard_map/all_gather | solution.py:76
  103.7 0.6 broadcast_in_dim.40
  104.3 17.5 %all-to-all-start.1 = ((f32[8,2,512]{2,1,0:T(2,128)}), f32[8,2,512]{2,1,0:T(2,128)S(1)}, u32[]{:S(2)}, u32[]{:S(2)}) async-start(f32[8,2,512]{2,1,0:T(2,128)} %broadcast_in_dim.40), calls=%async_computation.1 | async-start | bytes 65536 | tf_op jit(solution)/shard_map/all_to_all | solution.py:25
  121.9 4.7 %all-to-all-done.1 = f32[8,2,512]{2,1,0:T(2,128)S(1)} async-done(((f32[8,2,512]{2,1,0:T(2,128)}), f32[8,2,512]{2,1,0:T(2,128)S(1)}, u32[]{:S(2)}, u32[]{:S(2)}) %all-to-all-start.1) | async-done | bytes 32800 | tf_op jit(solution)/shard_map/all_to_all | solution.py:25
  126.9 23.7 %while.31 = (s32[]{:T(128)}, f32[512,512]{1,0:T(8,128)}, bf16[4,512,512]{1,2,0:T(8,128)(2,1)S(1)}, f32[]{:T(128)}, bf16[4,512,512]{2,1,0:T(8,128)(2,1)}, /*index...) while((s32[]{:T(128)}, f32[512,512]{1,0:T(8,128)}, ...), condition=%wide.region_16.17_spmd.clone, body=%wide.region_15.16_spmd.clone.sunk | while | flops 539230208 | bytes 5253747 | solution.py:202
  126.9 2.5 bitcast_dynamic-update-slice_fusion.2
  129.4 3.1 %fusion.82 = f32[512,512]{1,0:T(8,128)} fusion(bf16[512,512]{1,0:T(8,128)(2,1)S(1)} %get-tuple-element.337, f32[512,512]{1,0:T(8,128)} %get-tuple-element.380, f32[]{:T(128)} %get-tuple-element.392, pred[]{:T(512)S(6)} %compare.7, bf16[4,512,512]{2,1,0:T(8,128)(2,1)} %get-tuple-element.393, s32[]{:T(128)} %get-tuple-element.379), kind=kOutput, calls=%fused_computation.10.clone.1 | convolution fusion | flops 269221888 | bytes 3146753 | tf_op jit(solution)/shard_map/while/body/eval_jaxpr/dot_general | solution.py:197
  132.6 2.5 bitcast_dynamic-update-slice_fusion.2
  135.1 3.5 %fusion.82 = f32[512,512]{1,0:T(8,128)} fusion(bf16[512,512]{1,0:T(8,128)(2,1)S(1)} %get-tuple-element.337, f32[512,512]{1,0:T(8,128)} %get-tuple-element.380, f32[]{:T(128)} %get-tuple-element.392, pred[]{:T(512)S(6)} %compare.7, bf16[4,512,512]{2,1,0:T(8,128)(2,1)} %get-tuple-element.393, s32[]{:T(128)} %get-tuple-element.379), kind=kOutput, calls=%fused_computation.10.clone.1 | convolution fusion | flops 269221888 | bytes 3146753 | tf_op jit(solution)/shard_map/while/body/eval_jaxpr/dot_general | solution.py:197
  138.6 2.5 bitcast_dynamic-update-slice_fusion.2
  141.1 3.5 %fusion.82 = f32[512,512]{1,0:T(8,128)} fusion(bf16[512,512]{1,0:T(8,128)(2,1)S(1)} %get-tuple-element.337, f32[512,512]{1,0:T(8,128)} %get-tuple-element.380, f32[]{:T(128)} %get-tuple-element.392, pred[]{:T(512)S(6)} %compare.7, bf16[4,512,512]{2,1,0:T(8,128)(2,1)} %get-tuple-element.393, s32[]{:T(128)} %get-tuple-element.379), kind=kOutput, calls=%fused_computation.10.clone.1 | convolution fusion | flops 269221888 | bytes 3146753 | tf_op jit(solution)/shard_map/while/body/eval_jaxpr/dot_general | solution.py:197
  144.6 2.5 bitcast_dynamic-update-slice_fusion.2
  147.1 3.5 %fusion.82 = f32[512,512]{1,0:T(8,128)} fusion(bf16[512,512]{1,0:T(8,128)(2,1)S(1)} %get-tuple-element.337, f32[512,512]{1,0:T(8,128)} %get-tuple-element.380, f32[]{:T(128)} %get-tuple-element.392, pred[]{:T(512)S(6)} %compare.7, bf16[4,512,512]{2,1,0:T(8,128)(2,1)} %get-tuple-element.393, s32[]{:T(128)} %get-tuple-element.379), kind=kOutput, calls=%fused_computation.10.clone.1 | convolution fusion | flops 269221888 | bytes 3146753 | tf_op jit(solution)/shard_map/while/body/eval_jaxpr/dot_general | solution.py:197
  150.6 4.2 %convolution_multiply_fusion.3 = f32[2048,512]{1,0:T(8,128)} fusion(bf16[2048,512]{1,0:T(8,128)(2,1)S(1)} %bitcast.250, bf16[512,512]{1,0:T(8,128)(2,1)} %bitcast.2, f32[]{:T(128)} %bitcast.247), kind=kOutput, calls=%fused_computation.21 | convolution fusion | flops 1074790400 | bytes 6815748 | tf_op jit(solution)/shard_map/dot_general | solution.py:205
  154.9 51.6 %reduce-scatter.3.cloned.1.call-done = f32[256,512]{1,0:T(8,128)} async-done(((f32[2048,512]{1,0:T(8,128)}), f32[256,512]{1,0:T(8,128)}) %reduce-scatter.3.cloned.1.call-update) | async-done | bytes 524304 | tf_op jit(solution)/shard_map/reduce_scatter | solution.py:102
  206.6 5.0 %all-to-all-start.2 = ((f32[8,64,512]{2,1,0:T(8,128)}), f32[8,64,512]{2,1,0:T(8,128)S(1)}, u32[]{:S(2)}, u32[]{:S(2)}) async-start(f32[8,64,512]{2,1,0:T(8,128)} %bitcast.43), calls=%async_computation.2 | async-start | bytes 2097152 | tf_op jit(solution)/shard_map/all_to_all | solution.py:114
  212.2 14.5 %all-to-all-done.2 = f32[8,64,512]{2,1,0:T(8,128)S(1)} async-done(((f32[8,64,512]{2,1,0:T(8,128)}), f32[8,64,512]{2,1,0:T(8,128)S(1)}, u32[]{:S(2)}, u32[]{:S(2)}) %all-to-all-start.2) | async-done | bytes 1048608 | tf_op jit(solution)/shard_map/all_to_all | solution.py:114
  226.8 3.2 %reduce-scatter.5.cloned.1.call-done = f32[64,512]{1,0:T(8,128)} async-done(((f32[256,512]{1,0:T(8,128)}), f32[64,512]{1,0:T(8,128)}) %reduce-scatter.5.cloned.1.call-update) | async-done | bytes 131088 | tf_op jit(solution)/shard_map/reduce_scatter | solution.py:102
  230.0 1.2 multiply_reduce_fusion
  231.2 0.7 subtract_reduce_fusion
  233.2 0.8 dynamic-update-slice
  234.5 13.7 %all-reduce = f32[8]{0:T(128)S(1)} all-reduce(f32[8]{0:T(128)S(1)} %dynamic-update-slice), channel_id=1, replica_groups=mesh['row_0'=8,'row_1'=4,'col_0'=4,'col_1'=2] {'row_0'}, use_global_device_ids=true, to_apply=%add | all-reduce | flops 8 | bytes 64
  248.2 0.6 reduce_sum.131
  248.8 1.4 dynamic-update-slice.1
  250.8 6.8 %all-reduce.1 = f32[4]{0:T(128)S(1)} all-reduce(f32[4]{0:T(128)S(1)} %dynamic-update-slice.1), channel_id=1, replica_groups=mesh['row_0'=8,'row_1'=4,'col_0'=4,'col_1'=2] {'row_1'}, use_global_device_ids=true, to_apply=%add.1 | all-reduce | flops 4 | bytes 32
  257.6 0.6 reduce_sum.132
  258.2 1.4 dynamic-update-slice.2
  260.2 8.1 %all-reduce.2 = f32[4]{0:T(128)S(1)} all-reduce(f32[4]{0:T(128)S(1)} %dynamic-update-slice.2), channel_id=1, replica_groups=mesh['row_0'=8,'row_1'=4,'col_0'=4,'col_1'=2] {'col_0'}, use_global_device_ids=true, to_apply=%add.2 | all-reduce | flops 4 | bytes 32
  268.3 0.6 reduce_sum.133
  268.9 1.4 dynamic-update-slice.3
  270.3 12.1 %all-reduce.3 = f32[2]{0:T(128)S(1)} all-reduce(f32[2]{0:T(128)S(1)} %dynamic-update-slice.3), channel_id=1, replica_groups=mesh['row_0'=8,'row_1'=4,'col_0'=4,'col_1'=2] {'col_1'}, use_global_device_ids=true, to_apply=%add.3 | all-reduce | flops 2 | bytes 16
  282.4 0.8 subtract_divide_fusion.1
  284.4 1.7 subtract_divide_fusion
  (95 shorter events, 6.1 us)
Async XLA Ops:
  7.2 56.3 %all-gather.6.cloned.1.call-start = ((), (), s32[]{:S(2)}) async-start(), calls=%async_computation.5 | async-start | bytes 2359296 | tf_op jit(solution)/shard_map/all_gather | solution.py:34
  23.8 18.0 %all-to-all-start = ((bf16[8,64,512]{2,1,0:T(8,128)(2,1)}), bf16[8,64,512]{2,1,0:T(8,128)(2,1)}, u32[]{:S(2)}, u32[]{:S(2)}) async-start(bf16[8,64,512]{2,1,0:T(8,128)(2,1)} %broadcast_in_dim.39), calls=%async_computation | async-start | bytes 1048576 | tf_op jit(solution)/shard_map/all_to_all | solution.py:25
  104.3 22.2 %all-to-all-start.1 = ((f32[8,2,512]{2,1,0:T(2,128)}), f32[8,2,512]{2,1,0:T(2,128)S(1)}, u32[]{:S(2)}, u32[]{:S(2)}) async-start(f32[8,2,512]{2,1,0:T(2,128)} %broadcast_in_dim.40), calls=%async_computation.1 | async-start | bytes 65536 | tf_op jit(solution)/shard_map/all_to_all | solution.py:25
  121.8 84.7 %reduce-scatter.3.cloned.1.call-start = ((), (), s32[]{:S(2)}) async-start(), calls=%async_computation.6 | async-start | bytes 4718592 | tf_op jit(solution)/shard_map/reduce_scatter | solution.py:102
  154.8 56.8 %copy-start.5 = (u32[256]{0:T(256)S(1)}, u32[256]{0:T(256)}, u32[]{:S(2)}) copy-start(u32[256]{0:T(256)} %constant.73) | copy-start | bytes 3076
  154.8 75.2 %copy-start = (bf16[64,512]{1,0:T(8,128)(2,1)S(1)}, bf16[64,512]{1,0:T(8,128)(2,1)}, u32[]{:S(2)}) copy-start(bf16[64,512]{1,0:T(8,128)(2,1)} %param.8) | copy-start | bytes 196612
  154.9 75.2 %copy-start.1 = (bf16[64,512]{1,0:T(8,128)(2,1)S(1)}, bf16[64,512]{1,0:T(8,128)(2,1)}, u32[]{:S(2)}) copy-start(bf16[64,512]{1,0:T(8,128)(2,1)} %param.7) | copy-start | bytes 196612
  154.9 75.1 %reduce-scatter.5.cloned.1.call-start = ((), (), s32[]{:S(2)}) async-start(), calls=%async_computation.7 | async-start | bytes 655360 | tf_op jit(solution)/shard_map/reduce_scatter | solution.py:102
  206.5 27.4 %copy-start.4 = (u32[256]{0:T(256)S(1)}, u32[256]{0:T(256)}, u32[]{:S(2)}) copy-start(u32[256]{0:T(256)} %constant.78) | copy-start | bytes 3076
  206.5 43.7 %copy-start.3 = (u32[256]{0:T(256)S(1)}, u32[256]{0:T(256)}, u32[]{:S(2)}) copy-start(u32[256]{0:T(256)} %constant.83) | copy-start | bytes 3076
  206.6 53.1 %copy-start.2 = (u32[256]{0:T(256)S(1)}, u32[256]{0:T(256)}, u32[]{:S(2)}) copy-start(u32[256]{0:T(256)} %constant.88) | copy-start | bytes 3076
  206.6 20.1 %all-to-all-start.2 = ((f32[8,64,512]{2,1,0:T(8,128)}), f32[8,64,512]{2,1,0:T(8,128)S(1)}, u32[]{:S(2)}, u32[]{:S(2)}) async-start(f32[8,64,512]{2,1,0:T(8,128)} %bitcast.43), calls=%async_computation.2 | async-start | bytes 2097152 | tf_op jit(solution)/shard_map/all_to_all | solution.py:114
Sparse Core Ops, SparseCore 0:
  21.2 42.2 all-gather.5
  154.9 51.5 reduce-scatter.2
  209.0 20.9 reduce-scatter.4
